TPU v7x, 128 devices: a whole 4x4x4 slice. The times are simulated.
128 devices in a mesh: section: 4 (over x), zone: 32 (over z, y, core).
Axes of the slice: x: 4, y: 4, z: 4, core: 2. Of those that a mesh axis runs over, the one named last changes fastest.
Arguments:
- tiles: bfloat16 [4, 4096, 128, 128], P('section', 'zone'), may hold values from -0.5 to 0.5
- tile_row: int32 [4, 4096], P('section', 'zone'), may hold values from 0 to 19
- tile_col: int32 [4, 4096], P('section', 'zone'), may hold values from 0 to 63, as said below
- tile_live: int32 [4, 4096], P('section', 'zone'), may hold values from 0 to 1, as said below
- block_place: int32 [64], replicated, may hold values from 0 to 63, as said below
- demand: int32 [4, 81920, 128], P('section', 'zone'), may hold values from 0 to 15
- flow_cost: float32 [4, 8192], P('section', 'zone'), may hold values from -6 to 6
- stock_cost: float32 [4, 81920], P('section', 'zone'), may hold values from 0.1 to 1
- flows: float32 [4, 8192, 128], P('section', 'zone'), may hold values from 0 to 1
- stock: float32 [4, 81920, 128], P('section', 'zone'), may hold values from 0 to 2
- duals: float32 [4, 81920, 128], P('section', 'zone'), may hold values from -6 to 6
Outputs:
- flows_out: float32 [4, 8192, 128], P('section', 'zone')
- stock_out: float32 [4, 81920, 128], P('section', 'zone')
- duals_out: float32 [4, 81920, 128], P('section', 'zone')
Inputs may be any that keep to these rules, and one draw needn't show every extreme that they name: `tile_col`: flow block ids. For each phase and zone band, at most 4 live slots name flow blocks whose position // 2 is one given band; in each phase one band receives exactly 4 such slots from every zone band. `tile_live`: live flags of the slots, with the counts described for tile_col. `block_place`: A permutation of the flow blocks.
All inputs are finite; a program needn't handle non-finite values.
Results may differ from a plain program's by a relative error of at most 0.019.
Values may be sent and summed in bfloat16 or wider, within the bound.
A program may use at most 128 MiB of HBM per device.

v0:
```python
import jax
import jax.numpy as jnp
from jax import lax
from jax.sharding import PartitionSpec as P

ITERS = 2
STEP_PRIMAL = 0.25
STEP_DUAL = 0.25


def from_behind(value, axis, by):
    size = lax.axis_size(axis)
    return lax.ppermute(value, axis, [(i, (i + by) % size) for i in range(size)])


def per_device(
    tiles,
    tile_row,
    tile_col,
    tile_live,
    block_place,
    demand,
    flow_cost,
    stock_cost,
    flows,
    stock,
    duals,
):
    phase_count, slot_count, tile_size, unused_size = tiles.shape
    scenarios = flows.shape[2]
    zone_count = lax.axis_size("zone")
    blocks_total = block_place.shape[0]
    block_local = blocks_total // zone_count
    band_tiles = duals.shape[1] // tile_size
    width_flat = tile_size * scenarios
    alive = tile_live == 1
    position = block_place[tile_col]
    demand_rhs = demand.astype(jnp.float32) * 0.25
    phase_ids = jnp.arange(phase_count, dtype=jnp.int32)[:, None]
    block_ids = jnp.where(alive, position, -1)
    row_live = jnp.where(alive, tile_row, band_tiles)
    for iteration in range(ITERS):
        dual_half = duals.astype(jnp.bfloat16).reshape(
            phase_count, band_tiles, tile_size, scenarios
        )
        dual_picked = jnp.take_along_axis(dual_half, tile_row[:, :, None, None], axis=1)
        partial_value = jnp.einsum(
            "snij,snic->snjc", tiles, dual_picked, preferred_element_type=jnp.float32
        )
        partial_value = partial_value.astype(jnp.bfloat16).reshape(
            phase_count, slot_count, width_flat
        )
        shifted = jnp.where(block_ids >= 0, block_ids, -1)
        shifted = jnp.where(shifted < lax.axis_size("zone") * block_local, shifted, -1)

        def one_phase(values, segment_ids):
            return jax.ops.segment_sum(
                values.astype(jnp.float32),
                segment_ids,
                num_segments=lax.axis_size("zone") * block_local,
            )

        summed_blocks = jax.vmap(one_phase)(partial_value, shifted)
        summed = lax.psum_scatter(
            jnp.transpose(summed_blocks, (1, 0, 2)), "zone", scatter_dimension=0, tiled=True
        )
        pulled = jnp.transpose(summed, (1, 0, 2))
        pulled = pulled.reshape(phase_count, block_local * tile_size, scenarios)
        dual_edge = from_behind(duals, "section", -1)
        dual_after = jnp.concatenate([duals[1:], dual_edge], axis=0)
        new_flows = jnp.maximum(flows - STEP_PRIMAL * (flow_cost[:, :, None] - pulled), 0.0)
        new_stock = jnp.maximum(
            stock - STEP_PRIMAL * (stock_cost[:, :, None] - dual_after + duals), 0.0
        )
        flows_bar = (2.0 * new_flows - flows).astype(jnp.bfloat16)
        stock_bar = 2.0 * new_stock - stock
        gathered = lax.all_gather(flows_bar, "zone", axis=1, tiled=True).reshape(
            phase_count, blocks_total, tile_size, scenarios
        )
        flow_picked = jnp.take_along_axis(gathered, position[:, :, None, None], axis=1)
        products = jnp.einsum(
            "snij,snjc->snic", tiles, flow_picked, preferred_element_type=jnp.float32
        )
        pushed = (
            jnp.zeros((phase_count, band_tiles, tile_size, scenarios), jnp.float32)
            .at[phase_ids, row_live]
            .add(products, mode="drop")
        )
        pushed = pushed.reshape(phase_count, band_tiles * tile_size, scenarios)
        stock_edge = from_behind(stock_bar, "section", 1)
        stock_before = jnp.concatenate([stock_edge, stock_bar[:-1]], axis=0)
        duals = duals + STEP_DUAL * (demand_rhs - (pushed + stock_before - stock_bar))
        flows = new_flows
        stock = new_stock
    return (flows, stock, duals)


def solution(mesh):
    in_specs = (
        P("section", "zone", None, None),
        P("section", "zone"),
        P("section", "zone"),
        P("section", "zone"),
        P(),
        P("section", "zone", None),
        P("section", "zone"),
        P("section", "zone"),
        P("section", "zone", None),
        P("section", "zone", None),
        P("section", "zone", None),
    )
    out_specs = (P("section", "zone", None), P("section", "zone", None), P("section", "zone", None))
    return jax.shard_map(
        per_device, mesh=mesh, in_specs=in_specs, out_specs=out_specs, check_vma=False
    )
```

profile of v0, /device:TPU:1, one launch (start us, length us, event | category | flops | bytes accessed | tf_op | source)
XLA Modules:
  0.0 547.1 jit_solution(18323352815189189794)
XLA Ops:
  15.3 23.1 %collective-permute-done = f32[1,2560,128]{2,1,0:T(8,128)} collective-permute-done((f32[1,2560,128]{2,1,0:T(8,128)}, f32[1,2560,128]{2,1,0:T(8,128)}, u32[]{:S(2)}, u32[]{:S(2)}) %collective-permute-start) | collective-permute-done | bytes 1310752 | tf_op jit(solution)/shard_map/ppermute | solution.py:13
  38.4 4.0 multiply_subtract_fusion.1
  45.4 8.4 %convert_bitcast_fusion.1 = f32[128,128,128]{1,2,0:T(8,128)} fusion(bf16[1,128,128,128]{3,2,1,0:T(8,128)(2,1)} %param.15, bf16[128,128,128]{2,1,0:T(8,128)(2,1)} %gather_fusion.1, pred[128]{0:T(512)(128)(4,1)S(1)} %and_bitcast_fusion.1), kind=kOutput, calls=%fused_computation.10 | convolution fusion | flops 543162368 | bytes 16777344 | tf_op jit(solution)/shard_map/snij,snic->snjc/dot_general | solution.py:47
  53.8 9.4 %copy.35 = f32[128,128,128]{0,2,1:T(8,128)} copy(f32[128,128,128]{1,2,0:T(8,128)} %convert_bitcast_fusion.1) | data formatting | bytes 16777216 | tf_op jit(solution)/shard_map/vmap()/convert_element_type | solution.py:58
  63.2 9.0 %copy.36 = f32[128,16384]{1,0:T(8,128)} copy(f32[128,16384]{0,1:T(8,128)} %bitcast.163) | data formatting | bytes 16777216 | tf_op jit(solution)/shard_map/vmap()/convert_element_type | solution.py:58
  72.2 15.1 %scatter_custom_fusion.2 = f32[64,16384]{1,0:T(8,128)} fusion(s32[128]{0:T(128)S(1)} %fusion.51, f32[128,16384]{1,0:T(8,128)} %copy.36, f32[]{:T(128)} %constant.3.clone.1), kind=kCustom, calls=%fused_computation.39 | custom fusion | flops 2097152 | bytes 4194816 | tf_op jit(solution)/shard_map/vmap()/scatter-add | solution.py:57
  88.6 114.6 %all-reduce.6.cloned.1.call-done = f32[64,1,16384]{2,0,1:T(8,128)} async-done(((f32[64,1,16384]{2,0,1:T(8,128)}), f32[64,1,16384]{2,0,1:T(8,128)}) %all-reduce.6.cloned.1.call-update) | async-done | bytes 4194320
  207.1 42.9 %all-gather.3.cloned.1.call-done = bf16[1,8192,128]{2,1,0:T(8,128)(2,1)} async-done(((bf16[1,256,128]{2,1,0:T(8,128)(2,1)}), bf16[1,8192,128]{2,1,0:T(8,128)(2,1)}) %all-gather.3.cloned.1.call-update) | async-done | bytes 2097168 | tf_op jit(solution)/shard_map/all_gather | solution.py:77
  250.0 4.6 gather_fusion.2
  254.7 9.9 %fusion.20 = f32[128,128,128]{1,2,0:T(8,128)} fusion(bf16[1,128,128,128]{3,2,1,0:T(8,128)(2,1)} %param.15, bf16[128,128,128]{2,1,0:T(8,128)(2,1)} %gather_fusion.2, pred[128]{0:T(512)(128)(4,1)S(1)} %and_bitcast_fusion), kind=kOutput, calls=%fused_computation.31 | convolution fusion | flops 538968064 | bytes 16777344 | tf_op jit(solution)/shard_map/snij,snjc->snic/dot_general | solution.py:81
  264.6 9.0 %copy.38 = f32[128,128,128]{2,1,0:T(8,128)} copy(f32[128,128,128]{1,2,0:T(8,128)} %fusion.20) | data formatting | bytes 16777216 | tf_op jit(solution)/shard_map/snij,snjc->snic/dot_general | solution.py:81
  273.7 17.0 %scatter_fusion = f32[20,128,128]{2,1,0:T(8,128)S(1)} fusion(f32[20,128,128]{2,1,0:T(8,128)S(1)} %broadcast.166.clone, s32[128]{0:T(128)S(1)} %fusion.50, f32[128,128,128]{2,1,0:T(8,128)} %copy.38), kind=kCustom, calls=%fused_computation.5 | custom fusion | flops 2097152 | bytes 25166336 | tf_op jit(solution)/shard_map/scatter-add | solution.py:87
  296.9 8.4 %convert_bitcast_fusion = f32[128,128,128]{1,2,0:T(8,128)} fusion(bf16[1,128,128,128]{3,2,1,0:T(8,128)(2,1)} %param.15, bf16[128,128,128]{2,1,0:T(8,128)(2,1)} %gather_fusion.3, pred[128]{0:T(512)(128)(4,1)S(1)} %copy-done.9), kind=kOutput, calls=%fused_computation.9 | convolution fusion | flops 543162368 | bytes 16777344 | tf_op jit(solution)/shard_map/snij,snic->snjc/dot_general | solution.py:47
  305.2 9.4 %copy.40 = f32[128,128,128]{0,2,1:T(8,128)} copy(f32[128,128,128]{1,2,0:T(8,128)} %convert_bitcast_fusion) | data formatting | bytes 16777216 | tf_op jit(solution)/shard_map/vmap()/convert_element_type | solution.py:58
  314.6 9.0 %copy.41 = f32[128,16384]{1,0:T(8,128)} copy(f32[128,16384]{0,1:T(8,128)} %bitcast.164) | data formatting | bytes 16777216 | tf_op jit(solution)/shard_map/vmap()/convert_element_type | solution.py:58
  323.7 15.1 %scatter_custom_fusion.3 = f32[64,16384]{1,0:T(8,128)} fusion(s32[128]{0:T(128)} %copy-done.14, f32[128,16384]{1,0:T(8,128)} %copy.41, f32[]{:T(128)} %constant.3.clone.1), kind=kCustom, calls=%fused_computation.37 | custom fusion | flops 2097152 | bytes 4194816 | tf_op jit(solution)/shard_map/vmap()/scatter-add | solution.py:57
  338.8 110.8 %all-reduce.8.cloned.1.call-done = f32[64,1,16384]{2,0,1:T(8,128)} async-done(((f32[64,1,16384]{2,0,1:T(8,128)}), f32[64,1,16384]{2,0,1:T(8,128)}) %all-reduce.8.cloned.1.call-update) | async-done | bytes 4194320
  454.1 27.4 %collective-permute-done.2 = f32[1,2560,128]{2,1,0:T(8,128)S(1)} collective-permute-done((f32[1,2560,128]{2,1,0:T(8,128)S(1)}, f32[1,2560,128]{2,1,0:T(8,128)S(1)}, u32[]{:S(2)}, u32[]{:S(2)}) %collective-permute-start.2) | collective-permute-done | bytes 1310752 | tf_op jit(solution)/shard_map/ppermute | solution.py:13
  484.7 11.1 %all-gather.5.cloned.1.call-done = bf16[1,8192,128]{2,1,0:T(8,128)(2,1)} async-done(((bf16[1,256,128]{2,1,0:T(8,128)(2,1)}), bf16[1,8192,128]{2,1,0:T(8,128)(2,1)}) %all-gather.5.cloned.1.call-update) | async-done | bytes 2097168 | tf_op jit(solution)/shard_map/all_gather | solution.py:77
  495.8 4.8 gather_fusion.4
  500.5 9.9 %fusion.29 = f32[128,128,128]{1,2,0:T(8,128)} fusion(bf16[1,128,128,128]{3,2,1,0:T(8,128)(2,1)} %param.15, bf16[128,128,128]{2,1,0:T(8,128)(2,1)} %gather_fusion.4, pred[128]{0:T(512)(128)(4,1)S(1)} %copy-done.11), kind=kOutput, calls=%fused_computation.32 | convolution fusion | flops 538968064 | bytes 16777344 | tf_op jit(solution)/shard_map/snij,snjc->snic/dot_general | solution.py:81
  510.5 9.0 %copy.43 = f32[128,128,128]{2,1,0:T(8,128)} copy(f32[128,128,128]{1,2,0:T(8,128)} %fusion.29) | data formatting | bytes 16777216 | tf_op jit(solution)/shard_map/snij,snjc->snic/dot_general | solution.py:81
  519.6 17.0 %scatter_fusion.1 = f32[20,128,128]{2,1,0:T(8,128)S(1)} fusion(f32[20,128,128]{2,1,0:T(8,128)S(1)} %broadcast.166, s32[128]{0:T(128)S(1)} %copy-done.13, f32[128,128,128]{2,1,0:T(8,128)} %copy.43), kind=kCustom, calls=%fused_computation.6 | custom fusion | flops 2097152 | bytes 25166336 | tf_op jit(solution)/shard_map/scatter-add | solution.py:87
  536.6 3.7 fusion.45
  (73 shorter events, 29.6 us)
Async XLA Ops:
  7.2 4.1 copy-start
  7.2 196.0 %all-reduce.6.cloned.1.call-start = ((), (), s32[]{:S(2)}) async-start(), calls=%async_computation.2 | async-start | bytes 8388608
  7.2 31.1 %collective-permute-start = (f32[1,2560,128]{2,1,0:T(8,128)}, f32[1,2560,128]{2,1,0:T(8,128)}, u32[]{:S(2)}, u32[]{:S(2)}) collective-permute-start(f32[1,2560,128]{2,1,0:T(8,128)} %param.25), channel_id=1, source_target_pairs={{0,96},{32,0},{64,32},{96,64},{1,97},{33,1},{65,33},{97,65},{2,98}... | collective-permute-start | bytes 3932168 | tf_op jit(solution)/shard_map/ppermute | solution.py:13
  15.3 30.1 %copy-start.8 = (pred[128]{0:T(512)(128)(4,1)}, pred[128]{0:T(512)(128)(4,1)S(1)}, u32[]{:S(2)}) copy-start(pred[128]{0:T(512)(128)(4,1)S(1)} %and_bitcast_fusion.1) | copy-start | bytes 388
  15.3 56.9 %copy-start.14 = (s32[128]{0:T(128)}, s32[128]{0:T(128)S(1)}, u32[]{:S(2)}) copy-start(s32[128]{0:T(128)S(1)} %fusion.51) | copy-start | bytes 1540
  42.3 162.9 %copy-start.3 = (f32[1,2560,128]{2,1,0:T(8,128)}, f32[1,2560,128]{2,1,0:T(8,128)S(1)}, u32[]{:S(2)}) copy-start(f32[1,2560,128]{2,1,0:T(8,128)S(1)} %get-tuple-element.11) | copy-start | bytes 3932164
  72.2 15.2 %copy-start.15 = (u32[128]{0:T(128)S(1)}, u32[128]{0:T(128)}, u32[]{:S(2)}) copy-start(u32[128]{0:T(128)} %constant.66) | copy-start | bytes 1540
  72.2 132.2 %copy-start.4 = (f32[1,256,128]{2,1,0:T(8,128)S(1)}, f32[1,256,128]{2,1,0:T(8,128)}, u32[]{:S(2)}) copy-start(f32[1,256,128]{2,1,0:T(8,128)} %param.23) | copy-start | bytes 393220
  72.2 132.2 %copy-start.6 = (f32[1,256]{1,0:T(1,128)S(1)}, f32[1,256]{1,0:T(1,128)}, u32[]{:S(2)}) copy-start(f32[1,256]{1,0:T(1,128)} %param.21) | copy-start | bytes 3076
  87.3 162.7 %all-gather.3.cloned.1.call-start = ((), (), s32[]{:S(2)}) async-start(), calls=%async_computation | async-start | bytes 2162688 | tf_op jit(solution)/shard_map/all_gather | solution.py:77
  205.2 244.4 %all-reduce.8.cloned.1.call-start = ((), (), s32[]{:S(2)}) async-start(), calls=%async_computation.3 | async-start | bytes 8388608
  205.2 85.5 %collective-permute-start.1 = (f32[1,2560,128]{2,1,0:T(8,128)S(1)}, f32[1,2560,128]{2,1,0:T(8,128)}, u32[]{:S(2)}, u32[]{:S(2)}) collective-permute-start(f32[1,2560,128]{2,1,0:T(8,128)S(1)} %get-tuple-element.11), channel_id=1, source_target_pairs={{0,32},{32,64},{64,96},{96,0},{1,33},{33,65},{65,97},{97,1},{2,34}... | collective-permute-start | bytes 3932168 | tf_op jit(solution)/shard_map/ppermute | solution.py:13
  207.0 47.6 %copy-start.5 = (s32[1024]{0:T(1024)}, s32[1024]{0:T(1024)S(1)}, u32[]{:S(2)}) copy-start(s32[1024]{0:T(1024)S(1)} %pad_clamp_fusion) | copy-start | bytes 12292
  207.1 47.6 %copy-start.10 = (pred[128]{0:T(512)(128)(4,1)}, pred[128]{0:T(512)(128)(4,1)S(1)}, u32[]{:S(2)}) copy-start(pred[128]{0:T(512)(128)(4,1)S(1)} %and_bitcast_fusion) | copy-start | bytes 388
  207.1 66.6 %copy-start.12 = (s32[128]{0:T(128)}, s32[128]{0:T(128)S(1)}, u32[]{:S(2)}) copy-start(s32[128]{0:T(128)S(1)} %fusion.50) | copy-start | bytes 1540
  293.8 3.1 copy-start.9
  323.7 127.2 %copy-start.7 = (f32[1,256]{1,0:T(1,128)S(1)}, f32[1,256]{1,0:T(1,128)}, u32[]{:S(2)}) copy-start(f32[1,256]{1,0:T(1,128)} %param.21) | copy-start | bytes 3076
  323.7 157.9 %copy-start.2 = (f32[1,2560,128]{2,1,0:T(8,128)S(1)}, f32[1,2560,128]{2,1,0:T(8,128)}, u32[]{:S(2)}) copy-start(f32[1,2560,128]{2,1,0:T(8,128)} %get-tuple-element.12) | copy-start | bytes 3932164
  338.8 157.0 %all-gather.5.cloned.1.call-start = ((), (), s32[]{:S(2)}) async-start(), calls=%async_computation.1 | async-start | bytes 2162688 | tf_op jit(solution)/shard_map/all_gather | solution.py:77
  451.6 29.9 %collective-permute-start.2 = (f32[1,2560,128]{2,1,0:T(8,128)S(1)}, f32[1,2560,128]{2,1,0:T(8,128)S(1)}, u32[]{:S(2)}, u32[]{:S(2)}) collective-permute-start(f32[1,2560,128]{2,1,0:T(8,128)S(1)} %get-tuple-element.10), channel_id=1, source_target_pairs={{0,96},{32,0},{64,32},{96,64},{1,97},{33,1},{65,33},{97,65},{2,98}... | collective-permute-start | bytes 3932168 | tf_op jit(solution)/shard_map/ppermute | solution.py:13
  483.5 53.1 %collective-permute-start.3 = (f32[1,2560,128]{2,1,0:T(8,128)}, f32[1,2560,128]{2,1,0:T(8,128)}, u32[]{:S(2)}, u32[]{:S(2)}) collective-permute-start(f32[1,2560,128]{2,1,0:T(8,128)} %get-tuple-element.7), channel_id=1, source_target_pairs={{0,32},{32,64},{64,96},{96,0},{1,33},{33,65},{65,97},{97,1},{2,34}... | collective-permute-start | bytes 3932168 | tf_op jit(solution)/shard_map/ppermute | solution.py:13
  495.8 4.8 copy-start.11
  510.4 9.1 %copy-start.13 = (s32[128]{0:T(128)S(1)}, s32[128]{0:T(128)}, u32[]{:S(2)}) copy-start(s32[128]{0:T(128)} %copy-done.12) | copy-start | bytes 1540
  519.6 20.8 %copy-start.1 = (s32[64]{0:T(128)S(1)}, s32[64]{0:T(128)}, u32[]{:S(2)}) copy-start(s32[64]{0:T(128)} %param.19) | copy-start | bytes 772
Sparse Core Ops, SparseCore 0:
  87.4 115.7 all-reduce.5
  206.0 43.9 all-gather.2
  338.9 110.6 all-reduce.7
  451.8 43.9 all-gather.4
where the time goes:
time: 553 us; the launch traced here: 547 us
  waiting for transfers between devices  330 us (60%)
  other arithmetic  81.8 us (15%)
  local copies, waits for them, and re-layouts  74.9 us (14%)
  matrix products  36.6 us (7%)
  between operations  14.9 us (3%)
  starting transfers between devices  8.97 us (2%)
    unnamed x6, waiting for transfers between devices  225 us
    all_gather x2, waiting for transfers between devices, per_device(): lax.all_gather(flows_bar, 'zone', axis=1, tiled=True)  54 us
    ppermute x4, waiting for transfers between devices, from_behind(): lax.ppermute(value, axis, [(i, (i + by) % size) for i in range(size)])  50.5 us
    convert_element_type x4, local copies, waits for them, and re-layouts, one_phase(): values.astype(jnp.float32)  36.8 us
    scatter-add x2, other arithmetic, per_device(): pushed = jnp.zeros((phase_count, band_tiles, tile_size, scenarios), jnp.f...  34.1 us
    scatter-add x3, other arithmetic, one_phase(): jax.ops.segment_sum(values.astype(jnp.float32), segment_ids, num_segments...  30.2 us
    dot_general x2, matrix products, per_device(): jnp.einsum('snij,snjc->snic', tiles, flow_picked, preferred_element_type=...  19.8 us
    dot_general x2, local copies, waits for them, and re-layouts, per_device(): jnp.einsum('snij,snjc->snic', tiles, flow_picked, preferred_element_type=...  18 us
  transfers between devices with their start and end apart: 8, of which 6 were waited for; matrix products, arithmetic and copies ran while one was open for 16% of the time, Pallas kernels for 0%

commit v1 on v0

--- a/solution.py
+++ b/solution.py
@@ -1,3 +1,4 @@
+import functools
 import jax
 import jax.numpy as jnp
 from jax import lax
@@ -6,6 +7,16 @@
 ITERS = 2
 STEP_PRIMAL = 0.25
 STEP_DUAL = 0.25
+
+
+def begin_quotas_up(arr, which_dim):
+    t_next = jnp.stack([arr for _ in range(lax.axis_size("zone"))], axis=0)
+    u1 = lax.all_to_all(t_next, "zone", 0, 0)
+    y2 = jnp.concatenate(u1, which_dim)
+    return y2
+
+
+trace_the_ladders = functools.partial(begin_quotas_up, which_dim=1)
 
 
 def from_behind(value, axis, by):
@@ -74,7 +85,7 @@
         )
         flows_bar = (2.0 * new_flows - flows).astype(jnp.bfloat16)
         stock_bar = 2.0 * new_stock - stock
-        gathered = lax.all_gather(flows_bar, "zone", axis=1, tiled=True).reshape(
+        gathered = trace_the_ladders(flows_bar).reshape(
             phase_count, blocks_total, tile_size, scenarios
         )
         flow_picked = jnp.take_along_axis(gathered, position[:, :, None, None], axis=1)

time: 553 us -> 533 us (0.964)
  waiting for transfers between devices: 330 us -> 291 us
  starting transfers between devices: 8.97 us -> 20.6 us
    all_gather x2 -> x0, waiting for transfers between devices: 54 us -> none  [per_device(): lax.all_gather(flows_bar, 'zone', axis=1, tiled=True)]
    all_to_all x0 -> x2, waiting for transfers between devices: none -> 45.4 us  [begin_quotas_up(): u1 = lax.all_to_all(t_next, 'zone', 0, 0)]
    ppermute x4, waiting for transfers between devices: 50.5 us -> 22.5 us  [from_behind(): lax.ppermute(value, axis, [(i, (i + by) % size) for i in range(size)])]
    all_to_all x0 -> x2, starting transfers between devices: none -> 11.9 us  [begin_quotas_up(): u1 = lax.all_to_all(t_next, 'zone', 0, 0)]
    unnamed x6 -> x4, waiting for transfers between devices: 225 us -> 223 us
  transfers between devices with their start and end apart: 8 -> 8, of which waited for: 6 -> 5; matrix products, arithmetic and copies ran while one was open for 16% -> 18% of each run, Pallas kernels for 0% -> 0%
where the time goes in v1:
time: 533 us; the launch traced here: 526 us
  waiting for transfers between devices  291 us (55%)
  other arithmetic  86.3 us (16%)
  local copies, waits for them, and re-layouts  76 us (14%)
  matrix products  36.6 us (7%)
  starting transfers between devices  20.6 us (4%)
  between operations  15.2 us (3%)
    unnamed x4, waiting for transfers between devices  223 us
    all_to_all x2, waiting for transfers between devices, begin_quotas_up(): u1 = lax.all_to_all(t_next, 'zone', 0, 0)  45.4 us
    convert_element_type x4, local copies, waits for them, and re-layouts, one_phase(): values.astype(jnp.float32)  36.7 us
    scatter-add x2, other arithmetic, per_device(): pushed = jnp.zeros((phase_count, band_tiles, tile_size, scenarios), jnp.f...  34.1 us
    scatter-add x3, other arithmetic, one_phase(): jax.ops.segment_sum(values.astype(jnp.float32), segment_ids, num_segments...  30.3 us
    ppermute x4, waiting for transfers between devices, from_behind(): lax.ppermute(value, axis, [(i, (i + by) % size) for i in range(size)])  22.5 us
    dot_general x2, matrix products, per_device(): jnp.einsum('snij,snjc->snic', tiles, flow_picked, preferred_element_type=...  19.8 us
    dot_general x2, local copies, waits for them, and re-layouts, per_device(): jnp.einsum('snij,snjc->snic', tiles, flow_picked, preferred_element_type=...  17.9 us
  transfers between devices with their start and end apart: 8, of which 5 were waited for; matrix products, arithmetic and copies ran while one was open for 18% of the time, Pallas kernels for 0%

profile of v1, /device:TPU:1, one launch (start us, length us, event | category | flops | bytes accessed | tf_op | source)
XLA Modules:
  0.0 525.8 jit_solution(687811972024966198)
XLA Ops:
  15.9 22.5 %collective-permute-done = f32[1,2560,128]{2,1,0:T(8,128)S(1)} collective-permute-done((f32[1,2560,128]{2,1,0:T(8,128)}, f32[1,2560,128]{2,1,0:T(8,128)S(1)}, u32[]{:S(2)}, u32[]{:S(2)}) %collective-permute-start) | collective-permute-done | bytes 1310752 | tf_op jit(solution)/shard_map/ppermute | solution.py:24
  38.4 3.6 multiply_subtract_fusion.1
  45.0 8.4 %convert_bitcast_fusion.1 = f32[128,128,128]{1,2,0:T(8,128)} fusion(bf16[1,128,128,128]{3,2,1,0:T(8,128)(2,1)} %param.15, bf16[128,128,128]{2,1,0:T(8,128)(2,1)} %gather_fusion.1, pred[128]{0:T(512)(128)(4,1)S(1)} %and_bitcast_fusion.1), kind=kOutput, calls=%fused_computation.10 | convolution fusion | flops 543162368 | bytes 16777344 | tf_op jit(solution)/shard_map/snij,snic->snjc/dot_general | solution.py:58
  53.4 9.3 %copy.35 = f32[128,128,128]{0,2,1:T(8,128)} copy(f32[128,128,128]{1,2,0:T(8,128)} %convert_bitcast_fusion.1) | data formatting | bytes 16777216 | tf_op jit(solution)/shard_map/vmap()/convert_element_type | solution.py:69
  62.7 9.0 %copy.36 = f32[128,16384]{1,0:T(8,128)} copy(f32[128,16384]{0,1:T(8,128)} %bitcast.167) | data formatting | bytes 16777216 | tf_op jit(solution)/shard_map/vmap()/convert_element_type | solution.py:69
  71.7 15.3 %scatter_custom_fusion.2 = f32[64,16384]{1,0:T(8,128)} fusion(s32[128]{0:T(128)S(1)} %fusion.53, f32[128,16384]{1,0:T(8,128)} %copy.36, f32[]{:T(128)} %constant.3.clone.1), kind=kCustom, calls=%fused_computation.39 | custom fusion | flops 2097152 | bytes 4194816 | tf_op jit(solution)/shard_map/vmap()/scatter-add | solution.py:68
  88.4 114.5 %all-reduce.6.cloned.1.call-done = f32[64,1,16384]{2,0,1:T(8,128)} async-done(((f32[64,1,16384]{2,0,1:T(8,128)}), f32[64,1,16384]{2,0,1:T(8,128)}) %all-reduce.6.cloned.1.call-update) | async-done | bytes 4194320
  206.1 5.9 %all-to-all-start = ((bf16[32,1,256,128]{3,2,1,0:T(8,128)(2,1)}), bf16[32,1,256,128]{3,2,1,0:T(8,128)(2,1)S(1)}, u32[]{:S(2)}, u32[]{:S(2)}) async-start(bf16[32,1,256,128]{3,2,1,0:T(8,128)(2,1)} %stack.4), calls=%async_computation | async-start | bytes 4194304 | tf_op jit(solution)/shard_map/all_to_all | solution.py:14
  217.2 22.6 %all-to-all-done = bf16[32,1,256,128]{3,2,1,0:T(8,128)(2,1)S(1)} async-done(((bf16[32,1,256,128]{3,2,1,0:T(8,128)(2,1)}), bf16[32,1,256,128]{3,2,1,0:T(8,128)(2,1)S(1)}, u32[]{:S(2)}, u32[]{:S(2)}) %all-to-all-start) | async-done | bytes 2097184 | tf_op jit(solution)/shard_map/all_to_all | solution.py:14
  243.0 9.9 %fusion.20 = f32[128,128,128]{1,2,0:T(8,128)} fusion(bf16[1,128,128,128]{3,2,1,0:T(8,128)(2,1)} %param.15, bf16[128,128,128]{2,1,0:T(8,128)(2,1)} %gather_fusion.2, pred[128]{0:T(512)(128)(4,1)} %and_bitcast_fusion), kind=kOutput, calls=%fused_computation.31 | convolution fusion | flops 538968064 | bytes 16777344 | tf_op jit(solution)/shard_map/snij,snjc->snic/dot_general | solution.py:92
  252.9 9.0 %copy.38 = f32[128,128,128]{2,1,0:T(8,128)} copy(f32[128,128,128]{1,2,0:T(8,128)} %fusion.20) | data formatting | bytes 16777216 | tf_op jit(solution)/shard_map/snij,snjc->snic/dot_general | solution.py:92
  262.1 17.0 %scatter_fusion = f32[20,128,128]{2,1,0:T(8,128)S(1)} fusion(f32[20,128,128]{2,1,0:T(8,128)S(1)} %broadcast.172.clone, s32[128]{0:T(128)S(1)} %copy-done.10, f32[128,128,128]{2,1,0:T(8,128)} %copy.38), kind=kCustom, calls=%fused_computation.5 | custom fusion | flops 2097152 | bytes 25166336 | tf_op jit(solution)/shard_map/scatter-add | solution.py:98
  285.2 8.4 %convert_bitcast_fusion = f32[128,128,128]{1,2,0:T(8,128)} fusion(bf16[1,128,128,128]{3,2,1,0:T(8,128)(2,1)} %param.15, bf16[128,128,128]{2,1,0:T(8,128)(2,1)} %gather_fusion.3, pred[128]{0:T(512)(128)(4,1)S(1)} %copy-done.8), kind=kOutput, calls=%fused_computation.9 | convolution fusion | flops 543162368 | bytes 16777344 | tf_op jit(solution)/shard_map/snij,snic->snjc/dot_general | solution.py:58
  293.6 9.3 %copy.40 = f32[128,128,128]{0,2,1:T(8,128)} copy(f32[128,128,128]{1,2,0:T(8,128)} %convert_bitcast_fusion) | data formatting | bytes 16777216 | tf_op jit(solution)/shard_map/vmap()/convert_element_type | solution.py:69
  302.9 9.0 %copy.41 = f32[128,16384]{1,0:T(8,128)} copy(f32[128,16384]{0,1:T(8,128)} %bitcast.168) | data formatting | bytes 16777216 | tf_op jit(solution)/shard_map/vmap()/convert_element_type | solution.py:69
  311.9 15.0 %scatter_custom_fusion.3 = f32[64,16384]{1,0:T(8,128)} fusion(s32[128]{0:T(128)} %copy-done.13, f32[128,16384]{1,0:T(8,128)} %copy.41, f32[]{:T(128)} %constant.3.clone.1), kind=kCustom, calls=%fused_computation.37 | custom fusion | flops 2097152 | bytes 4194816 | tf_op jit(solution)/shard_map/vmap()/scatter-add | solution.py:68
  329.3 108.6 %all-reduce.8.cloned.1.call-done = f32[64,1,16384]{2,0,1:T(8,128)} async-done(((f32[64,1,16384]{2,0,1:T(8,128)}), f32[64,1,16384]{2,0,1:T(8,128)}) %all-reduce.8.cloned.1.call-update) | async-done | bytes 4194320
  441.8 5.9 %all-to-all-start.1 = ((bf16[32,1,256,128]{3,2,1,0:T(8,128)(2,1)}), bf16[32,1,256,128]{3,2,1,0:T(8,128)(2,1)S(1)}, u32[]{:S(2)}, u32[]{:S(2)}) async-start(bf16[32,1,256,128]{3,2,1,0:T(8,128)(2,1)} %stack.5), calls=%async_computation.1 | async-start | bytes 4194304 | tf_op jit(solution)/shard_map/all_to_all | solution.py:14
  447.7 3.6 multiply_subtract_fusion
  452.8 22.8 %all-to-all-done.1 = bf16[32,1,256,128]{3,2,1,0:T(8,128)(2,1)S(1)} async-done(((bf16[32,1,256,128]{3,2,1,0:T(8,128)(2,1)}), bf16[32,1,256,128]{3,2,1,0:T(8,128)(2,1)S(1)}, u32[]{:S(2)}, u32[]{:S(2)}) %all-to-all-start.1) | async-done | bytes 2097184 | tf_op jit(solution)/shard_map/all_to_all | solution.py:14
  478.9 9.9 %fusion.29 = f32[128,128,128]{1,2,0:T(8,128)} fusion(bf16[1,128,128,128]{3,2,1,0:T(8,128)(2,1)} %param.15, bf16[128,128,128]{2,1,0:T(8,128)(2,1)} %gather_fusion.4, pred[128]{0:T(512)(128)(4,1)S(1)} %copy-done.9), kind=kOutput, calls=%fused_computation.32 | convolution fusion | flops 538968064 | bytes 16777344 | tf_op jit(solution)/shard_map/snij,snjc->snic/dot_general | solution.py:92
  488.8 9.0 %copy.43 = f32[128,128,128]{2,1,0:T(8,128)} copy(f32[128,128,128]{1,2,0:T(8,128)} %fusion.29) | data formatting | bytes 16777216 | tf_op jit(solution)/shard_map/snij,snjc->snic/dot_general | solution.py:92
  497.9 17.0 %scatter_fusion.1 = f32[20,128,128]{2,1,0:T(8,128)S(1)} fusion(f32[20,128,128]{2,1,0:T(8,128)S(1)} %broadcast.172, s32[128]{0:T(128)S(1)} %copy-done.11, f32[128,128,128]{2,1,0:T(8,128)} %copy.43), kind=kCustom, calls=%fused_computation.6 | custom fusion | flops 2097152 | bytes 25166336 | tf_op jit(solution)/shard_map/scatter-add | solution.py:98
  515.0 3.7 fusion.45
  (71 shorter events, 41.2 us)
Async XLA Ops:
  7.2 4.1 copy-start
  7.2 195.7 %all-reduce.6.cloned.1.call-start = ((), (), s32[]{:S(2)}) async-start(), calls=%async_computation.2 | async-start | bytes 8388608
  7.2 31.1 %collective-permute-start = (f32[1,2560,128]{2,1,0:T(8,128)}, f32[1,2560,128]{2,1,0:T(8,128)S(1)}, u32[]{:S(2)}, u32[]{:S(2)}) collective-permute-start(f32[1,2560,128]{2,1,0:T(8,128)} %param.25), channel_id=1, source_target_pairs={{0,96},{32,0},{64,32},{96,64},{1,97},{33,1},{65,33},{97,65},{2,98}... | collective-permute-start | bytes 3932168 | tf_op jit(solution)/shard_map/ppermute | solution.py:24
  12.5 3.3 copy-start.12
  15.8 29.2 %copy-start.7 = (pred[128]{0:T(512)(128)(4,1)}, pred[128]{0:T(512)(128)(4,1)S(1)}, u32[]{:S(2)}) copy-start(pred[128]{0:T(512)(128)(4,1)S(1)} %and_bitcast_fusion.1) | copy-start | bytes 388
  15.8 55.9 %copy-start.13 = (s32[128]{0:T(128)}, s32[128]{0:T(128)S(1)}, u32[]{:S(2)}) copy-start(s32[128]{0:T(128)S(1)} %fusion.53) | copy-start | bytes 1540
  42.0 170.1 %copy-start.2 = (f32[1,2560,128]{2,1,0:T(8,128)}, f32[1,2560,128]{2,1,0:T(8,128)S(1)}, u32[]{:S(2)}) copy-start(f32[1,2560,128]{2,1,0:T(8,128)S(1)} %get-tuple-element.11) | copy-start | bytes 3932164
  71.7 15.3 %copy-start.14 = (u32[128]{0:T(128)S(1)}, u32[128]{0:T(128)}, u32[]{:S(2)}) copy-start(u32[128]{0:T(128)} %constant.66) | copy-start | bytes 1540
  71.7 132.4 %copy-start.3 = (f32[1,256,128]{2,1,0:T(8,128)S(1)}, f32[1,256,128]{2,1,0:T(8,128)}, u32[]{:S(2)}) copy-start(f32[1,256,128]{2,1,0:T(8,128)} %param.23) | copy-start | bytes 393220
  71.7 132.4 %copy-start.5 = (f32[1,256]{1,0:T(1,128)S(1)}, f32[1,256]{1,0:T(1,128)}, u32[]{:S(2)}) copy-start(f32[1,256]{1,0:T(1,128)} %param.21) | copy-start | bytes 3076
  206.1 33.8 %all-to-all-start = ((bf16[32,1,256,128]{3,2,1,0:T(8,128)(2,1)}), bf16[32,1,256,128]{3,2,1,0:T(8,128)(2,1)S(1)}, u32[]{:S(2)}, u32[]{:S(2)}) async-start(bf16[32,1,256,128]{3,2,1,0:T(8,128)(2,1)} %stack.4), calls=%async_computation | async-start | bytes 4194304 | tf_op jit(solution)/shard_map/all_to_all | solution.py:14
  212.0 226.0 %all-reduce.8.cloned.1.call-start = ((), (), s32[]{:S(2)}) async-start(), calls=%async_computation.3 | async-start | bytes 8388608
  212.1 67.0 %collective-permute-start.1 = (f32[1,2560,128]{2,1,0:T(8,128)S(1)}, f32[1,2560,128]{2,1,0:T(8,128)}, u32[]{:S(2)}, u32[]{:S(2)}) collective-permute-start(f32[1,2560,128]{2,1,0:T(8,128)S(1)} %get-tuple-element.11), channel_id=1, source_target_pairs={{0,32},{32,64},{64,96},{96,0},{1,33},{33,65},{65,97},{97,1},{2,34}... | collective-permute-start | bytes 3932168 | tf_op jit(solution)/shard_map/ppermute | solution.py:24
  252.9 9.1 %copy-start.10 = (s32[128]{0:T(128)S(1)}, s32[128]{0:T(128)}, u32[]{:S(2)}) copy-start(s32[128]{0:T(128)} %fusion.52) | copy-start | bytes 1540
  282.1 3.1 copy-start.8
  311.9 127.3 %copy-start.4 = (f32[1,256,128]{2,1,0:T(8,128)S(1)}, f32[1,256,128]{2,1,0:T(8,128)}, u32[]{:S(2)}) copy-start(f32[1,256,128]{2,1,0:T(8,128)} %param.23) | copy-start | bytes 393220
  311.9 127.3 %copy-start.6 = (f32[1,256]{1,0:T(1,128)S(1)}, f32[1,256]{1,0:T(1,128)}, u32[]{:S(2)}) copy-start(f32[1,256]{1,0:T(1,128)} %param.21) | copy-start | bytes 3076
  326.9 120.8 %collective-permute-start.2 = (f32[1,2560,128]{2,1,0:T(8,128)S(1)}, f32[1,2560,128]{2,1,0:T(8,128)}, u32[]{:S(2)}, u32[]{:S(2)}) collective-permute-start(f32[1,2560,128]{2,1,0:T(8,128)S(1)} %get-tuple-element.10), channel_id=1, source_target_pairs={{0,96},{32,0},{64,32},{96,64},{1,97},{33,1},{65,33},{97,65},{2,98}... | collective-permute-start | bytes 3932168 | tf_op jit(solution)/shard_map/ppermute | solution.py:24
  441.8 33.8 %all-to-all-start.1 = ((bf16[32,1,256,128]{3,2,1,0:T(8,128)(2,1)}), bf16[32,1,256,128]{3,2,1,0:T(8,128)(2,1)S(1)}, u32[]{:S(2)}, u32[]{:S(2)}) async-start(bf16[32,1,256,128]{3,2,1,0:T(8,128)(2,1)} %stack.5), calls=%async_computation.1 | async-start | bytes 4194304 | tf_op jit(solution)/shard_map/all_to_all | solution.py:14
  451.4 63.6 %collective-permute-start.3 = (f32[1,2560,128]{2,1,0:T(8,128)}, f32[1,2560,128]{2,1,0:T(8,128)}, u32[]{:S(2)}, u32[]{:S(2)}) collective-permute-start(f32[1,2560,128]{2,1,0:T(8,128)} %get-tuple-element.7), channel_id=1, source_target_pairs={{0,32},{32,64},{64,96},{96,0},{1,33},{33,65},{65,97},{97,1},{2,34}... | collective-permute-start | bytes 3932168 | tf_op jit(solution)/shard_map/ppermute | solution.py:24
  475.6 3.3 copy-start.9
  488.8 9.1 %copy-start.11 = (s32[128]{0:T(128)S(1)}, s32[128]{0:T(128)}, u32[]{:S(2)}) copy-start(s32[128]{0:T(128)} %fusion.52) | copy-start | bytes 1540
  497.9 20.8 %copy-start.1 = (s32[64]{0:T(128)S(1)}, s32[64]{0:T(128)}, u32[]{:S(2)}) copy-start(s32[64]{0:T(128)} %param.19) | copy-start | bytes 772
Sparse Core Ops, SparseCore 0:
  87.2 115.6 all-reduce.5
  327.0 110.9 all-reduce.7
